TPU v7x, 512 devices: a whole 4x8x8 slice. The times are simulated.
512 devices in a mesh: seq: 128 (over z, x, y_hi, core), grp: 4 (over y_lo).
Axes of the slice: x: 4, y: 8 (y_hi: 2, y_lo: 4; y = y_hi * 4 + y_lo), z: 8, core: 2. Of those that a mesh axis runs over, the one named last changes fastest.
Arguments:
- signal: bfloat16 [4, 131072, 384], P('grp', 'seq'), may hold values from -6 to 6
- tap_weights: bfloat16 [3, 384, 384], replicated, may hold values from -0.1875 to 0.1875
- bias_inner: float32 [384], replicated, may hold values from -3 to 3
- w_out: bfloat16 [384, 384], replicated, may hold values from -0.3125 to 0.3125
- cotangent: bfloat16 [4, 131072, 384], P('grp', 'seq'), may hold values from -6 to 6
Outputs:
- output: bfloat16 [4, 131072, 384], P('grp', 'seq')
- grad_signal: bfloat16 [4, 131072, 384], P('grp', 'seq')
- grad_taps: bfloat16 [3, 384, 384], replicated
- grad_bias: float32 [384], replicated
- grad_out: bfloat16 [384, 384], replicated
All inputs are finite; a program needn't handle non-finite values.
Results may differ from a plain program's by a relative error of at most 0.0075.
Values may be sent and summed in bfloat16 or wider, within the bound.
A program may use at most 64 MiB of HBM per device.

v0:
```python
import math

import jax
import jax.numpy as jnp
from jax import lax
from jax.sharding import PartitionSpec as P


def shifted(value, axis, steps):
    count = lax.axis_size(axis)
    first, last = (max(0, -steps), min(count, count - steps))
    return lax.ppermute(value, axis, [(source, source + steps) for source in range(first, last)])


def gelu_exact(value):
    return value * 0.5 * (1.0 + jax.scipy.special.erf(value / math.sqrt(2.0)))


def gelu_slope(value):
    normal_cdf = 0.5 * (1.0 + jax.scipy.special.erf(value / math.sqrt(2.0)))
    return normal_cdf + value * jnp.exp(-0.5 * value * value) / math.sqrt(2.0 * math.pi)


def shards(signal, tap_weights, bias_inner, w_out, cotangent):
    wide_sig = signal[0].astype(jnp.float32)
    cot_rows = cotangent[0]
    gelu_output = gelu_exact(wide_sig).astype(jnp.bfloat16)
    leading_rows = shifted(gelu_output, "seq", 4)
    trailing_rows = shifted(gelu_output, "seq", -4)
    pre_gate = bias_inner + jnp.dot(gelu_output, tap_weights[1], preferred_element_type=jnp.float32)
    pre_gate = pre_gate + jnp.dot(leading_rows, tap_weights[0], preferred_element_type=jnp.float32)
    pre_gate = pre_gate + jnp.dot(trailing_rows, tap_weights[2], preferred_element_type=jnp.float32)
    hidden = gelu_exact(pre_gate).astype(jnp.bfloat16)
    output = (wide_sig + jnp.dot(hidden, w_out, preferred_element_type=jnp.float32)).astype(
        jnp.bfloat16
    )
    grad_hidden = jnp.dot(cot_rows, w_out.T, preferred_element_type=jnp.float32)
    preactivation_gradient = (grad_hidden * gelu_slope(pre_gate)).astype(jnp.bfloat16)
    first_term = jnp.dot(
        preactivation_gradient, tap_weights[0].T, preferred_element_type=jnp.float32
    )
    last_term = jnp.dot(
        preactivation_gradient, tap_weights[2].T, preferred_element_type=jnp.float32
    )
    activation_gradient = jnp.dot(
        preactivation_gradient, tap_weights[1].T, preferred_element_type=jnp.float32
    )
    activation_gradient = activation_gradient + shifted(
        first_term.astype(jnp.bfloat16), "seq", -4
    ).astype(first_term.dtype)
    activation_gradient = activation_gradient + shifted(
        last_term.astype(jnp.bfloat16), "seq", 4
    ).astype(last_term.dtype)
    grad_signal = (
        cot_rows.astype(jnp.float32) + activation_gradient * gelu_slope(wide_sig)
    ).astype(jnp.bfloat16)
    tap_local = jnp.stack(
        [
            jnp.dot(leading_rows.T, preactivation_gradient, preferred_element_type=jnp.float32),
            jnp.dot(gelu_output.T, preactivation_gradient, preferred_element_type=jnp.float32),
            jnp.dot(trailing_rows.T, preactivation_gradient, preferred_element_type=jnp.float32),
        ],
        0,
    )
    out_local = jnp.dot(hidden.T, cot_rows, preferred_element_type=jnp.float32)
    bias_local = jnp.sum(preactivation_gradient.astype(jnp.float32), 0)
    tap_total, bias_total, out_total = lax.psum((tap_local, bias_local, out_local), ("seq", "grp"))
    return (
        output[None],
        grad_signal[None],
        tap_total.astype(jnp.bfloat16),
        bias_total,
        out_total.astype(jnp.bfloat16),
    )


def solution(mesh):
    return jax.shard_map(
        shards,
        mesh=mesh,
        in_specs=(P("grp", "seq", None), P(), P(), P(), P("grp", "seq", None)),
        out_specs=(P("grp", "seq", None), P("grp", "seq", None), P(), P(), P()),
        check_vma=False,
    )
```

profile of v0, /device:TPU:1, one launch (start us, length us, event | category | flops | bytes accessed | tf_op | source)
XLA Modules:
  0.0 171.0 jit_solution(12844385995635504639)
XLA Ops:
  0.6 0.0 copy-start
  0.6 0.0 copy-start.1
  0.7 1.6 fusion.13
  2.2 0.0 copy-start.2
  2.2 4.1 %collective-permute-start = (bf16[1024,384]{1,0:T(8,128)(2,1)S(1)}, bf16[1024,384]{1,0:T(8,128)(2,1)S(1)}, u32[]{:S(2)}, u32[]{:S(2)}) collective-permute-start(bf16[1024,384]{1,0:T(8,128)(2,1)S(1)} %fusion.13), channel_id=1, source_target_pairs={{0,16},{4,20},{8,24},{12,28},{16,32},{20,36},{24,40},{28,44},{32,4... | collective-permute-start | bytes 2359304 | tf_op jit(solution)/shard_map/ppermute | solution.py:12
  6.4 1.3 collective-permute-start.1
  7.7 0.0 copy-done.1
  7.7 1.6 fusion.29
  9.3 0.0 copy-start.3
  9.3 9.9 %collective-permute-done = bf16[1024,384]{1,0:T(8,128)(2,1)S(1)} collective-permute-done((bf16[1024,384]{1,0:T(8,128)(2,1)S(1)}, bf16[1024,384]{1,0:T(8,128)(2,1)S(1)}, u32[]{:S(2)}, u32[]{:S(2)}) %collective-permute-start) | collective-permute-done | bytes 786464 | tf_op jit(solution)/shard_map/ppermute | solution.py:12
  19.2 0.0 copy-done.2
  19.2 0.6 fusion.47
  19.8 0.0 copy-start.4
  19.8 3.2 %collective-permute-done.1 = bf16[1024,384]{1,0:T(8,128)(2,1)S(1)} collective-permute-done((bf16[1024,384]{1,0:T(8,128)(2,1)S(1)}, bf16[1024,384]{1,0:T(8,128)(2,1)S(1)}, u32[]{:S(2)}, u32[]{:S(2)}) %collective-permute-start.1) | collective-permute-done | bytes 786464 | tf_op jit(solution)/shard_map/ppermute | solution.py:12
  23.1 0.0 copy-done.3
  23.1 0.8 multiply_convert_fusion
  23.9 0.0 copy-done
  24.0 1.1 convert_reduce_fusion
  25.0 0.6 convolution_bitcast_fusion.1
  25.6 1.5 convolution_convert_fusion
  27.2 1.5 convolution_convert_fusion.1
  28.7 0.6 convolution_bitcast_fusion
  29.3 0.6 convolution_bitcast_fusion.2
  29.9 0.1 pad_maximum_fusion
  30.0 0.6 fusion.31
  30.6 1.3 collective-permute-start.2
  31.9 7.9 %collective-permute-start.3 = (bf16[1024,384]{1,0:T(8,128)(2,1)}, bf16[1024,384]{1,0:T(8,128)(2,1)}, u32[]{:S(2)}, u32[]{:S(2)}) collective-permute-start(bf16[1024,384]{1,0:T(8,128)(2,1)} %convolution_convert_fusion), channel_id=1, source_target_pairs={{0,16},{4,20},{8,24},{12,28},{16,32},{20,36},{24,40},{28,44},{32,4... | collective-permute-start | bytes 2359304 | tf_op jit(solution)/shard_map/ppermute | solution.py:12
  39.8 1.5 fusion.27
  41.3 125.5 %all-reduce.2 = (bf16[3,384,384]{2,1,0:T(8,128)(2,1)}, f32[384]{0:T(512)}, bf16[384,384]{1,0:T(8,128)(2,1)}) all-reduce(f32[3,384,384]{2,1,0:T(8,128)S(1)} %pad_maximum_fusion, f32[384]{0:T(512)S(1)} %get-tuple-element.10, f32[384,384]{1,0:T(8,128)S(1)} %fusion.31), channel_id=1, replica_groups=mesh['seq'=128,'grp'=4] {'seq','grp'}, use_global_device_ids=true, to_apply=%region_0.0 | all-reduce | flops 590208 | bytes 3542016 | tf_op jit(solution)/shard_map/psum | solution.py:67
  166.9 0.0 collective-permute-done.2
  166.9 0.0 collective-permute-done.3
  166.9 4.2 %fusion.40 = bf16[1,1024,384]{2,1,0:T(8,128)(2,1)} fusion(bf16[1,1024,384]{2,1,0:T(8,128)(2,1)} %param.5, bf16[1024,384]{1,0:T(8,128)(2,1)} %collective-permute-done.3, bf16[1024,384]{1,0:T(8,128)(2,1)} %collective-permute-done.2, bf16[1,1024,384]{2,1,0:T(8,128)(2,1)} %param.9, bf16[1024,384]{1,0:T(8,128)(2,1)S(1)} %get-tuple-element.11, ...), kind=kOutput, calls=%fused_computation.51 | convolution fusion | flops 308674560 | bytes 5013504 | tf_op jit(solution)/shard_map/dot_general | solution.py:45
  (1 shorter events, 0.0 us)
Async XLA Ops:
  0.6 23.3 %copy-start = (bf16[384,384]{1,0:T(8,128)(2,1)S(1)}, bf16[384,384]{1,0:T(8,128)(2,1)}, u32[]{:S(2)}) copy-start(bf16[384,384]{1,0:T(8,128)(2,1)} %param.8) | copy-start | bytes 884740
  0.6 7.0 %copy-start.1 = (bf16[1,1024,384]{2,1,0:T(8,128)(2,1)S(1)}, bf16[1,1024,384]{2,1,0:T(8,128)(2,1)}, u32[]{:S(2)}) copy-start(bf16[1,1024,384]{2,1,0:T(8,128)(2,1)} %param.5) | copy-start | bytes 2359300
  2.2 17.0 %copy-start.2 = (bf16[3,384,384]{2,1,0:T(8,128)(2,1)S(1)}, bf16[3,384,384]{2,1,0:T(8,128)(2,1)}, u32[]{:S(2)}) copy-start(bf16[3,384,384]{2,1,0:T(8,128)(2,1)} %param.6) | copy-start | bytes 2654212
  2.2 17.0 %collective-permute-start = (bf16[1024,384]{1,0:T(8,128)(2,1)S(1)}, bf16[1024,384]{1,0:T(8,128)(2,1)S(1)}, u32[]{:S(2)}, u32[]{:S(2)}) collective-permute-start(bf16[1024,384]{1,0:T(8,128)(2,1)S(1)} %fusion.13), channel_id=1, source_target_pairs={{0,16},{4,20},{8,24},{12,28},{16,32},{20,36},{24,40},{28,44},{32,4... | collective-permute-start | bytes 2359304 | tf_op jit(solution)/shard_map/ppermute | solution.py:12
  6.4 16.7 %collective-permute-start.1 = (bf16[1024,384]{1,0:T(8,128)(2,1)S(1)}, bf16[1024,384]{1,0:T(8,128)(2,1)S(1)}, u32[]{:S(2)}, u32[]{:S(2)}) collective-permute-start(bf16[1024,384]{1,0:T(8,128)(2,1)S(1)} %fusion.13), channel_id=1, source_target_pairs={{16,0},{20,4},{24,8},{28,12},{32,16},{36,20},{40,24},{44,28},{48,3... | collective-permute-start | bytes 2359304 | tf_op jit(solution)/shard_map/ppermute | solution.py:12
  9.3 13.8 %copy-start.3 = (f32[384]{0:T(512)S(1)}, f32[384]{0:T(512)}, u32[]{:S(2)}) copy-start(f32[384]{0:T(512)} %param.7) | copy-start | bytes 4612
  19.8 4.1 %copy-start.4 = (bf16[1,1024,384]{2,1,0:T(8,128)(2,1)S(1)}, bf16[1,1024,384]{2,1,0:T(8,128)(2,1)}, u32[]{:S(2)}) copy-start(bf16[1,1024,384]{2,1,0:T(8,128)(2,1)} %param.9) | copy-start | bytes 2359300
  30.6 136.2 %collective-permute-start.2 = (bf16[1024,384]{1,0:T(8,128)(2,1)}, bf16[1024,384]{1,0:T(8,128)(2,1)}, u32[]{:S(2)}, u32[]{:S(2)}) collective-permute-start(bf16[1024,384]{1,0:T(8,128)(2,1)} %convolution_convert_fusion.1), channel_id=1, source_target_pairs={{16,0},{20,4},{24,8},{28,12},{32,16},{36,20},{40,24},{44,28},{48,3... | collective-permute-start | bytes 2359304 | tf_op jit(solution)/shard_map/ppermute | solution.py:12
  31.9 134.9 %collective-permute-start.3 = (bf16[1024,384]{1,0:T(8,128)(2,1)}, bf16[1024,384]{1,0:T(8,128)(2,1)}, u32[]{:S(2)}, u32[]{:S(2)}) collective-permute-start(bf16[1024,384]{1,0:T(8,128)(2,1)} %convolution_convert_fusion), channel_id=1, source_target_pairs={{0,16},{4,20},{8,24},{12,28},{16,32},{20,36},{24,40},{28,44},{32,4... | collective-permute-start | bytes 2359304 | tf_op jit(solution)/shard_map/ppermute | solution.py:12
where the time goes:
time: 171 us
  blocking collectives  126 us (74%)
  matrix products  15.3 us (9%)
  starting transfers between devices  14.6 us (9%)
  waiting for transfers between devices  13.1 us (8%)
    psum x1, blocking collectives, shards(): lax.psum((tap_local, bias_local, out_local), ('seq', 'grp'))  126 us
    ppermute x4, starting transfers between devices, shifted(): lax.ppermute(value, axis, [(source, source + steps) for source in range(f...  14.6 us
    ppermute x4, waiting for transfers between devices, shifted(): lax.ppermute(value, axis, [(source, source + steps) for source in range(f...  13.1 us
    dot_general x1, matrix products, shards(): jnp.dot(preactivation_gradient, tap_weights[1].T, preferred_element_type=...  4.16 us
  transfers between devices with their start and end apart: 4, of which 2 were waited for; matrix products, arithmetic and copies ran while one was open for 2% of the time, Pallas kernels for 0%

commit v1 on v0

v1 whole, which is shorter than its diff:
```python
import functools
import math

import jax
import jax.numpy as jnp
from jax import lax
from jax.experimental import pallas as pl
from jax.experimental.pallas import tpu as pltpu
from jax.sharding import PartitionSpec as P

F32 = jnp.float32
BF16 = jnp.bfloat16
MESH = pl.DeviceIdType.MESH

NX = 4
NYH = 2
CHUNK = 128
SHARE = 48


def rows_dot(a, b):
    return lax.dot_general(a, b, (((1,), (0,)), ((), ())), preferred_element_type=F32)


def rows_dot_t(a, b):
    return lax.dot_general(a, b, (((1,), (1,)), ((), ())), preferred_element_type=F32)


def sum_rows_dot(a, b):
    return lax.dot_general(a, b, (((0,), (0,)), ((), ())), preferred_element_type=F32)


def cdf_of(v):
    return 0.5 * (1.0 + lax.erf(v * (1.0 / math.sqrt(2.0))))


def slope_of(v, cdf):
    return cdf + v * jnp.exp(-0.5 * v * v) * (1.0 / math.sqrt(2.0 * math.pi))


class Half:
    def __init__(self, start, piece, n_first, n_second, extra):
        self.start, self.piece = start, piece
        self.n_first, self.n_second = n_first, n_second
        pieces = piece // 8
        owners = max(n for n in range(1, n_second + 1 - extra) if pieces % n == 0)
        self.owned = piece // owners
        self.weight_owners = owners
        self.owners = owners + extra


def kernel(cfg, *refs):
    nz, ny, nyl, nc, ch, halves = cfg
    (sig_h, taps_h, bias_r, wout_h, cot_h, out_h, gsig_h, gtaps_h, gbias_r, gout_h,
     sig, cot, taps, wout, act, lead, trail, gp, gpl, gpr, outb, gsb, pre, gh, slope,
     acc, bacc, cs, cr, bcr, s1s_a, s1s_b, s1r_a, s1r_b, b1r, p_a, p_b, s2r_a, s2r_b, xs_a, xs_b, pf_a, pf_b, bfin, gall,
     in_sem, w_sem, out_sem, act_s, act_r, gp_s, gp_r, c_s, c_r, s1_s, s1_r, b1_s, b1_r, s2_s, s2_r,
     x_s, x_r, ag2_s, ag2_r, ag1_s, ag1_r, bag_s, bag_r, cag_s, cag_r) = refs
    s1s, s1r, pp, s2r, xs, pf = (s1s_a, s1s_b), (s1r_a, s1r_b), (p_a, p_b), (s2r_a, s2r_b), (xs_a, xs_b), (pf_a, pf_b)
    seq, grp = lax.axis_index("seq"), lax.axis_index("grp")
    hop = 2 * NYH
    core = seq % 2
    y = ((seq // 2) % NYH) * nyl + grp
    x = (seq // hop) % NX
    z = seq // (hop * NX)
    n_seq = nz * NX * hop
    has_right = seq + hop < n_seq
    has_left = seq >= hop
    right, left = (seq + hop, grp), (seq - hop, grp)
    other = (seq + 1 - 2 * core, grp)

    def y_peer(p):
        return (seq + (p // nyl - (seq // 2) % NYH) * 2, p % nyl)

    def z_peer(p):
        return (seq + (p - z) * (hop * NX), grp)

    def x_peer(p):
        return (seq + (p - x) * hop, grp)

    first, second = (y_peer, z_peer), (z_peer, y_peer)
    me_first, me_second = (y, z), (z, y)

    def remote(src, dst, send_sem, recv_sem, to):
        return pltpu.make_async_remote_copy(src_ref=src, dst_ref=dst, send_sem=send_sem, recv_sem=recv_sem,
                                            device_id=to, device_id_type=MESH)

    def ring(n, me, body):
        def step(k, carry):
            body(lax.rem(me + k, n))
            return carry
        lax.fori_loop(1, n, step, 0)

    def chunks(first_c, last_c, body):
        def step(c, carry):
            body(c)
            return carry
        lax.fori_loop(first_c, last_c, step, 0)

    def sig_copy(c):
        return pltpu.make_async_copy(sig_h.at[0, pl.ds(pl.multiple_of(c * ch, ch), ch)], sig.at[c], in_sem.at[c])

    def cot_copy(c):
        return pltpu.make_async_copy(cot_h.at[0, pl.ds(pl.multiple_of(c * ch, ch), ch)], cot.at[c], in_sem.at[nc + c])

    taps_copy = pltpu.make_async_copy(taps_h, taps, w_sem.at[0])
    wout_copy = pltpu.make_async_copy(wout_h, wout, w_sem.at[1])
    chunks(0, nc, lambda c: sig_copy(c).start())
    taps_copy.start()
    wout_copy.start()
    chunks(0, nc, lambda c: cot_copy(c).start())

    barrier = pltpu.get_barrier_semaphore()

    def greet(to):
        pl.semaphore_signal(barrier, inc=1, device_id=to, device_id_type=MESH)

    cross_right = jnp.logical_and(x == NX - 1, has_right)
    cross_left = jnp.logical_and(x == 0, has_left)
    ring(NX, x, lambda p: greet(x_peer(p)))
    pl.when(cross_right)(lambda: greet(right))
    pl.when(cross_left)(lambda: greet(left))
    greet(other)
    ring(ny, y, lambda p: greet(y_peer(p)))
    ring(nz, z, lambda p: greet(z_peer(p)))
    greeted = 1 + (NX - 1) + (ny - 1) + (nz - 1)

    def activate(c):
        sig_copy(c).wait()
        v = sig[c].astype(F32)
        act[c] = (v * cdf_of(v)).astype(BF16)

    def act_right(c):
        return remote(act.at[c], lead.at[c], act_s.at[c], act_r.at[c], right)

    def act_left(c):
        return remote(act.at[c], trail.at[c], act_s.at[nc + c], act_r.at[nc + c], left)

    def act_send(c):
        pl.when(has_right)(lambda: act_right(c).start())
        pl.when(has_left)(lambda: act_left(c).start())

    def gp_right(c):
        return remote(gp.at[c], gpl.at[c], gp_s.at[c], gp_r.at[c], right)

    def gp_left(c):
        return remote(gp.at[c], gpr.at[c], gp_s.at[nc + c], gp_r.at[nc + c], left)

    def gp_send(c):
        pl.when(has_right)(lambda: gp_right(c).start())
        pl.when(has_left)(lambda: gp_left(c).start())

    activate(0)
    pl.semaphore_wait(barrier, greeted + jnp.where(cross_right, 1, 0) + jnp.where(cross_left, 1, 0))
    act_send(0)

    def activate_send(c):
        activate(c)
        act_send(c)

    chunks(1, nc, activate_send)

    @pl.when(jnp.logical_not(has_left))
    def _():
        lead[...] = jnp.zeros_like(lead)
        gpl[...] = jnp.zeros_like(gpl)

    @pl.when(jnp.logical_not(has_right))
    def _():
        trail[...] = jnp.zeros_like(trail)
        gpr[...] = jnp.zeros_like(gpr)

    acc[...] = jnp.zeros_like(acc)
    bacc[...] = jnp.zeros_like(bacc)
    bias = bias_r[...].reshape(1, -1)
    taps_copy.wait()
    wout_copy.wait()

    def prepare(c):
        cot_copy(c).wait()
        pre[c] = bias + rows_dot(act[c], taps[1])
        gh[c] = rows_dot_t(cot[c], wout[...])
        v = sig[c].astype(F32)
        slope[c] = slope_of(v, cdf_of(v))

    chunks(0, nc, prepare)

    def act_wait(c):
        pl.when(has_left)(lambda: act_right(c).wait_recv())
        pl.when(has_right)(lambda: act_left(c).wait_recv())

    def out_copy(c):
        return pltpu.make_async_copy(outb.at[c], out_h.at[0, pl.ds(pl.multiple_of(c * ch, ch), ch)], out_sem.at[c])

    def gsig_copy(c):
        return pltpu.make_async_copy(gsb.at[c], gsig_h.at[0, pl.ds(pl.multiple_of(c * ch, ch), ch)], out_sem.at[nc + c])

    n_in = taps.shape[1]

    def add_rows(k, value):
        acc[k // 2, pl.ds((k % 2) * n_in, n_in)] += value

    def work(c):
        lead_c, trail_c, act_c, cot_c = lead[c], trail[c], act[c], cot[c]
        v = pre[c] + rows_dot(lead_c, taps[0]) + rows_dot(trail_c, taps[2])
        cdf = cdf_of(v)
        hidden = (v * cdf).astype(BF16)
        grad = (gh[c] * slope_of(v, cdf)).astype(BF16)
        gp[c] = grad
        outb[c] = (sig[c].astype(F32) + rows_dot(hidden, wout[...])).astype(BF16)
        out_copy(c).start()
        add_rows(0, sum_rows_dot(lead_c, grad))
        add_rows(1, sum_rows_dot(act_c, grad))
        add_rows(2, sum_rows_dot(trail_c, grad))
        add_rows(3, sum_rows_dot(hidden, cot_c))
        wide = grad.astype(F32)
        bacc[...] += jnp.sum(wide.reshape(ch // 8, 8, wide.shape[-1]), 0)

    def wait_work(c):
        act_wait(c)
        work(c)

    chunks(0, nc - 1, wait_work)
    act_wait(nc - 1)
    chunks(0, nc - 1, gp_send)
    work(nc - 1)
    gp_send(nc - 1)

    def core_copy(h):
        rows = pl.ds(halves[h].start, halves[h].piece * halves[h].n_first)
        return remote(cs.at[rows], cr.at[rows], c_s.at[h], c_r.at[h], other)

    bias_core = remote(bacc, bcr, c_s.at[2], c_r.at[2], other)
    for h in range(2):
        rows = pl.ds(halves[h].start, halves[h].piece * halves[h].n_first)
        cs[rows] = acc[1 - core, rows].astype(BF16)
        core_copy(h).start()
    bias_core.start()

    zb = nz - 1

    def s1_copy(h, p, sender):
        return remote(s1s[h].at[p], s1r[h].at[sender], s1_s.at[h, p], s1_r.at[h, sender], first[h](p))

    def b1_copy(sender):
        return remote(bfin.at[0], b1r.at[sender], b1_s, b1_r.at[sender], z_peer(zb))

    for h in range(2):
        core_copy(h).wait_recv()
        hf = halves[h]

        def add_piece(p, h=h, hf=hf):
            rows = pl.ds(pl.multiple_of(hf.start + p * hf.piece, 16), hf.piece)
            total = acc[core, rows] + cr[rows].astype(F32)
            acc[core, rows] = total
            s1s[h][p] = total.astype(BF16)

        def add_send(p, h=h):
            add_piece(p)
            s1_copy(h, p, me_first[h]).start()

        ring(hf.n_first, me_first[h], add_send)
        add_piece(me_first[h])
    bias_core.wait_recv()
    bfin[0] = bacc[...] + bcr[...]
    pl.when(z != zb)(lambda: b1_copy(z).start())

    def adjoint(c):
        pl.when(has_left)(lambda: gp_right(c).wait_recv())
        pl.when(has_right)(lambda: gp_left(c).wait_recv())
        grad = rows_dot_t(gp[c], taps[1]) + rows_dot_t(gpr[c], taps[0]) + rows_dot_t(gpl[c], taps[2])
        gsb[c] = (cot[c].astype(F32) + grad * slope[c]).astype(BF16)
        gsig_copy(c).start()

    chunks(0, 3, adjoint)

    def s2_copy(h, q, sender):
        n = halves[h].owned
        return remote(pp[h].at[pl.ds(pl.multiple_of(q * n, 8), n)], s2r[h].at[sender], s2_s.at[h, q], s2_r.at[h, sender], second[h](q))

    for h in range(2):
        hf = halves[h]
        rows = pl.ds(pl.multiple_of(hf.start + me_first[h] * hf.piece, 16), hf.piece)
        pp[h][pl.ds(0, hf.piece)] = acc[core, rows]

        def take(p, h=h, hf=hf):
            s1_copy(h, me_first[h], p).wait_recv()
            pp[h][pl.ds(0, hf.piece)] += s1r[h][p].astype(F32)

        ring(hf.n_first, me_first[h], take)
        if hf.owners > hf.weight_owners:
            spare = pl.ds(hf.piece, hf.owned)
            pp[h][spare] = jnp.zeros((hf.owned, acc.shape[-1]), F32)

            @pl.when(z == zb)
            def _(h=h, hf=hf):
                head = pl.ds(hf.piece, 8)
                pp[h][head] = bfin[0]

                def take_bias(p):
                    b1_copy(p).wait_recv()
                    pp[h][head] += b1r[p]

                ring(nz, z, take_bias)

        def scatter(q, h=h, hf=hf):
            pl.when(q < hf.owners)(lambda: s2_copy(h, q, me_second[h]).start())

        ring(hf.n_second, me_second[h], scatter)

    def x_copy(h, p, sender):
        return remote(xs[h].at[sender], xs[h].at[sender], x_s.at[h, p], x_r.at[h, sender], x_peer(p))

    for h in range(2):
        hf = halves[h]

        @pl.when(me_second[h] < hf.owners)
        def _(h=h, hf=hf):
            rows = pl.ds(pl.multiple_of(me_second[h] * hf.owned, 8), hf.owned)
            xs[h][x] = pp[h][rows]

            def take(p):
                s2_copy(h, me_second[h], p).wait_recv()
                xs[h][x] += s2r[h][p]

            ring(hf.n_second, me_second[h], take)
            ring(NX, x, lambda p: x_copy(h, p, x).start())

    def ag2_copy(h, p, sender):
        n = halves[h].owned
        rows = pl.ds(pl.multiple_of(sender * n, 8), n)
        return remote(pf[h].at[rows], pf[h].at[rows], ag2_s.at[h, p], ag2_r.at[h, sender], second[h](p))

    for h in range(2):
        hf = halves[h]

        @pl.when(me_second[h] < hf.owners)
        def _(h=h, hf=hf):
            ring(NX, x, lambda p: x_copy(h, x, p).wait_recv())
            total = xs[h][0]
            for p in range(1, NX):
                total = total + xs[h][p]
            pf[h][pl.ds(pl.multiple_of(me_second[h] * hf.owned, 8), hf.owned)] = total
            ring(hf.n_second, me_second[h], lambda p: ag2_copy(h, p, me_second[h]).start())

    def piece_of(h, p):
        return pl.ds(pl.multiple_of(halves[h].start + p * halves[h].piece, 16), halves[h].piece)

    def ag1_copy(h, p, sender):
        ref = gall.at[core, piece_of(h, sender)]
        return remote(ref, ref, ag1_s.at[h, p], ag1_r.at[h, sender], first[h](p))

    def cag_copy(h, p, side):
        ref = gall.at[side, piece_of(h, p)]
        return remote(ref, ref, cag_s.at[h, p], cag_r.at[h, p], other)

    def bag_copy(p):
        return remote(bfin.at[1], bfin.at[1], bag_s.at[p], bag_r, z_peer(p))

    for h in range(2):
        hf = halves[h]

        def take(q, h=h, hf=hf):
            pl.when(q < hf.owners)(lambda: ag2_copy(h, me_second[h], q).wait_recv())

        ring(hf.n_second, me_second[h], take)
        gall[core, piece_of(h, me_first[h])] = pf[h][pl.ds(0, hf.piece)].astype(BF16)
        ring(hf.n_first, me_first[h], lambda p, h=h: ag1_copy(h, p, me_first[h]).start())
        cag_copy(h, me_first[h], core).start()
        if hf.owners > hf.weight_owners:

            @pl.when(z == zb)
            def _(h=h, hf=hf):
                bfin[1] = pf[h][pl.ds(hf.piece, 8)]
                ring(nz, z, lambda p: bag_copy(p).start())

    chunks(3, nc, adjoint)

    for h in range(2):
        hf = halves[h]

        def pass_on(p, h=h):
            ag1_copy(h, me_first[h], p).wait_recv()
            cag_copy(h, p, core).start()

        ring(hf.n_first, me_first[h], pass_on)
    pl.when(z != zb)(lambda: bag_copy(z).wait_recv())
    gbias_r[...] = jnp.sum(bfin[1], 0)
    for h in range(2):
        hf = halves[h]
        chunks(0, hf.n_first, lambda p, h=h: cag_copy(h, p, 1 - core).wait_recv())
    grad_copies = [
        pltpu.make_async_copy(gall.at[k // 2, pl.ds((k % 2) * n_in, n_in)], gtaps_h.at[k] if k < 3 else gout_h, w_sem.at[2 + k])
        for k in range(4)
    ]
    for copy in grad_copies:
        copy.start()

    def sent(c):
        @pl.when(has_right)
        def _():
            act_right(c).wait_send()
            gp_right(c).wait_send()

        @pl.when(has_left)
        def _():
            act_left(c).wait_send()
            gp_left(c).wait_send()

        out_copy(c).wait()
        gsig_copy(c).wait()

    chunks(0, nc, sent)
    bias_core.wait_send()
    pl.when(z != zb)(lambda: b1_copy(z).wait_send())
    pl.when(z == zb)(lambda: ring(nz, z, lambda p: bag_copy(p).wait_send()))
    for h in range(2):
        hf = halves[h]
        core_copy(h).wait_send()

        def sent_first(p, h=h):
            s1_copy(h, p, me_first[h]).wait_send()
            ag1_copy(h, p, me_first[h]).wait_send()

        ring(hf.n_first, me_first[h], sent_first)
        chunks(0, hf.n_first, lambda p, h=h: cag_copy(h, p, core).wait_send())

        def sent_second(q, h=h, hf=hf):
            pl.when(q < hf.owners)(lambda: s2_copy(h, q, me_second[h]).wait_send())

        ring(hf.n_second, me_second[h], sent_second)

        @pl.when(me_second[h] < hf.owners)
        def _(h=h, hf=hf):
            ring(NX, x, lambda p: x_copy(h, p, x).wait_send())
            ring(hf.n_second, me_second[h], lambda p: ag2_copy(h, p, me_second[h]).wait_send())

    for copy in grad_copies:
        copy.wait()


def shards(sizes, signal, tap_weights, bias_inner, w_out, cotangent):
    n_seq, nyl = sizes
    nz, ny = n_seq // (2 * NYH * NX), NYH * nyl
    _, rows, c = signal.shape
    taps, _, hid = tap_weights.shape
    ch = CHUNK
    nc = rows // ch
    core_rows = (taps + 1) * c // 2
    share = SHARE * 8 // ny
    halves = (
        Half(0, share, ny, nz, 0),
        Half(share * ny, (core_rows - share * ny) // nz, nz, ny, 1),
    )
    cfg = (nz, ny, nyl, nc, ch, halves)
    any_spec = pl.BlockSpec(memory_space=pl.ANY)
    vmem_spec = pl.BlockSpec(memory_space=pltpu.VMEM)
    block = lambda dtype: pltpu.VMEM((nc, ch, c), dtype)
    dma = lambda *shape: pltpu.SemaphoreType.DMA(shape)
    most = max(ny, nz)
    ha, hb = halves
    scratch = [
        block(BF16), block(BF16), pltpu.VMEM(tap_weights.shape, BF16), pltpu.VMEM(w_out.shape, BF16),
        *[block(BF16)] * 8,
        block(F32), block(F32), block(F32),
        pltpu.VMEM((2, core_rows, hid), F32), pltpu.VMEM((8, hid), F32),
        pltpu.VMEM((core_rows, hid), BF16), pltpu.VMEM((core_rows, hid), BF16), pltpu.VMEM((8, hid), F32),
        *[pltpu.VMEM((h.n_first, h.piece, hid), BF16) for h in halves],
        *[pltpu.VMEM((h.n_first, h.piece, hid), BF16) for h in halves],
        pltpu.VMEM((nz, 8, hid), F32),
        *[pltpu.VMEM((h.owners * h.owned, hid), F32) for h in halves],
        *[pltpu.VMEM((h.n_second, h.owned, hid), F32) for h in halves],
        *[pltpu.VMEM((NX, h.owned, hid), F32) for h in halves],
        *[pltpu.VMEM((h.owners * h.owned, hid), F32) for h in halves],
        pltpu.VMEM((2, 8, hid), F32),
        pltpu.VMEM((2, core_rows, hid), BF16),
        dma(2 * nc), dma(6), dma(2 * nc),
        dma(2 * nc), dma(2 * nc), dma(2 * nc), dma(2 * nc),
        dma(3), dma(3), dma(2, most), dma(2, most), pltpu.SemaphoreType.DMA, dma(nz), dma(2, most), dma(2, most),
        dma(2, NX), dma(2, NX), dma(2, most), dma(2, most), dma(2, most), dma(2, most),
        dma(nz), pltpu.SemaphoreType.DMA, dma(2, most), dma(2, most),
    ]
    return pl.pallas_call(
        functools.partial(kernel, cfg),
        out_shape=(
            jax.ShapeDtypeStruct(signal.shape, BF16),
            jax.ShapeDtypeStruct(signal.shape, BF16),
            jax.ShapeDtypeStruct(tap_weights.shape, BF16),
            jax.ShapeDtypeStruct((hid,), F32),
            jax.ShapeDtypeStruct(w_out.shape, BF16),
        ),
        in_specs=[any_spec, any_spec, vmem_spec, any_spec, any_spec],
        out_specs=(any_spec, any_spec, any_spec, vmem_spec, any_spec),
        scratch_shapes=scratch,
        compiler_params=pltpu.CompilerParams(collective_id=0, has_side_effects=True, vmem_limit_bytes=48 * 1024 * 1024),
    )(signal, tap_weights, bias_inner, w_out, cotangent)


def solution(mesh):
    sizes = (mesh.shape["seq"], mesh.shape["grp"])
    return jax.shard_map(
        functools.partial(shards, sizes),
        mesh=mesh,
        in_specs=(P("grp", "seq", None), P(), P(), P(), P("grp", "seq", None)),
        out_specs=(P("grp", "seq", None), P("grp", "seq", None), P(), P(), P()),
        check_vma=False,
    )
```

time: 171 us -> 98.3 us (0.57)
  blocking collectives: 126 us -> 0 us
  Pallas kernels: 0 us -> 88.3 us
  matrix products: 15.3 us -> 0 us
  starting transfers between devices: 14.6 us -> 0 us
  waiting for transfers between devices: 13.1 us -> 0 us
  local copies, waits for them, and re-layouts: 0.03 us -> 9.03 us
    psum x1 -> x0, blocking collectives: 126 us -> none  [shards(): lax.psum((tap_local, bias_local, out_local), ('seq', 'grp'))]
    pallas_call x0 -> x1, Pallas kernels: none -> 88.3 us  [shards(): pl.pallas_call(functools.partial(kernel, cfg), out_shape=(jax.ShapeDtypeS...]
    dot_general x12 -> x0, matrix products: 15.3 us -> none  [the longest x1 4.16 us: shards(): jnp.dot(preactivation_gradient, tap_weights[1].T, preferred_element_type=...]
    ppermute x4 -> x0, starting transfers between devices: 14.6 us -> none  [shifted(): lax.ppermute(value, axis, [(source, source + steps) for source in range(f...]
    ppermute x4 -> x0, waiting for transfers between devices: 13.1 us -> none  [shifted(): lax.ppermute(value, axis, [(source, source + steps) for source in range(f...]
    unnamed x10 -> x15, local copies, waits for them, and re-layouts: 0.03 us -> 9.03 us
  transfers between devices with their start and end apart: 4 -> 0, of which waited for: 2 -> 0; matrix products, arithmetic and copies ran while one was open for 2% -> 0% of each run, Pallas kernels for 0% -> 0%
where the time goes in v1:
time: 98.3 us; the launch traced here: 98 us
  Pallas kernels  88.3 us (90%)
  local copies, waits for them, and re-layouts  9.03 us (9%)
    pallas_call x1, Pallas kernels, shards(): pl.pallas_call(functools.partial(kernel, cfg), out_shape=(jax.ShapeDtypeS...  88.3 us
    unnamed x15, local copies, waits for them, and re-layouts  9.03 us

profile of v1, /device:TPU:1, one launch (start us, length us, event | category | flops | bytes accessed | tf_op | source)
XLA Modules:
  0.0 98.0 jit_solution(14928125420355440119)
XLA Ops:
  0.6 0.0 copy-start
  0.6 1.2 %copy-done = bf16[3,384,384]{2,1,0:T(8,128)(2,1)S(1)} copy-done((bf16[3,384,384]{2,1,0:T(8,128)(2,1)S(1)}, bf16[3,384,384]{2,1,0:T(8,128)(2,1)}, u32[]{:S(2)}) %copy-start) | copy-done | bytes 884760
  1.8 0.0 copy-start.1
  1.8 1.1 %copy-done.1 = bf16[1,1024,384]{2,1,0:T(8,128)(2,1)S(1)} copy-done((bf16[1,1024,384]{2,1,0:T(8,128)(2,1)S(1)}, bf16[1,1024,384]{2,1,0:T(8,128)(2,1)}, u32[]{:S(2)}) %copy-start.1) | copy-done | bytes 786456
  2.9 0.0 copy-start.2
  2.9 1.1 %copy-done.2 = bf16[1,1024,384]{2,1,0:T(8,128)(2,1)S(1)} copy-done((bf16[1,1024,384]{2,1,0:T(8,128)(2,1)S(1)}, bf16[1,1024,384]{2,1,0:T(8,128)(2,1)}, u32[]{:S(2)}) %copy-start.2) | copy-done | bytes 786456
  4.1 0.0 copy-start.3
  4.1 1.0 copy-done.3
  5.0 0.0 copy-start.4
  5.0 0.7 copy-done.4
  5.7 88.3 %shard_map.92 = (bf16[1,1024,384]{2,1,0:T(8,128)(2,1)S(1)}, bf16[1,1024,384]{2,1,0:T(8,128)(2,1)S(1)}, bf16[3,384,384]{2,1,0:T(8,128)(2,1)S(1)}, f32[384]{0:T(512)S(1)}, bf16[384,384]{1,0:T(8,128)(2,1)S(1)}) custom-call(bf16[1,1024,384]{2,1,0:T(8,128)(2,1)S(1)} %copy-done.1, bf16[3,384,384]{2,1,0:T(8,128)(2,1)S(1)} %copy-done, f32[384]{0:T(512)S(1)} %copy-done.4, ...), custom_call_target="tpu_custom_call" | custom-call | tf_op jit(solution)/shard_map/pallas_call | solution.py:483
  94.0 0.9 copy.15
  94.9 0.9 copy.16
  95.8 0.9 copy.17
  96.7 0.6 copy.18
  97.3 0.7 copy.19
Async XLA Ops:
  0.6 1.2 %copy-start = (bf16[3,384,384]{2,1,0:T(8,128)(2,1)S(1)}, bf16[3,384,384]{2,1,0:T(8,128)(2,1)}, u32[]{:S(2)}) copy-start(bf16[3,384,384]{2,1,0:T(8,128)(2,1)} %refs_1_.1) | copy-start | bytes 2654212
  1.8 1.1 %copy-start.1 = (bf16[1,1024,384]{2,1,0:T(8,128)(2,1)S(1)}, bf16[1,1024,384]{2,1,0:T(8,128)(2,1)}, u32[]{:S(2)}) copy-start(bf16[1,1024,384]{2,1,0:T(8,128)(2,1)} %refs_0_.1) | copy-start | bytes 2359300
  2.9 1.1 %copy-start.2 = (bf16[1,1024,384]{2,1,0:T(8,128)(2,1)S(1)}, bf16[1,1024,384]{2,1,0:T(8,128)(2,1)}, u32[]{:S(2)}) copy-start(bf16[1,1024,384]{2,1,0:T(8,128)(2,1)} %refs_4_.1) | copy-start | bytes 2359300
  4.1 1.0 copy-start.3
  5.0 0.7 copy-start.4
